TPU v7x, 32 devices: a whole 2x2x4 slice. The times are simulated.
32 devices in a mesh: groups: 2 (over y), expert: 4 (over z), tensor: 4 (over x, core).
Axes of the slice: x: 2, y: 2, z: 4, core: 2. Of those that a mesh axis runs over, the one named last changes fastest.
Arguments:
- source_states: bfloat16 [2048, 2048], P(('groups', 'expert')), parts along dimension 0, may hold values from -6 to 6
- routes: int32 [2048, 2], P(('groups', 'expert')), parts along dimension 0, may hold values from 0 to 3, all different within a row; in each aligned block of 256 rows (0 to 255, 256 to 511, ...) at most 256 rows name the same one
- router_weight: bfloat16 [2048, 4], replicated, may hold values from -0.125 to 0.125
- fc1_weight: bfloat16 [4, 2048, 8192], P('expert', None, 'tensor'), may hold values from -0.125 to 0.125
- fc2_weight: bfloat16 [4, 8192, 2048], P('expert', 'tensor'), may hold values from -0.09375 to 0.09375
- lengths: int32 [8, 8], P(('groups', 'expert')), parts along dimension 0, may hold values from 1 to 48, 256 in all within a row
- lang_ids: int32 [64, 6], P(('groups', 'expert')), parts along dimension 0, may hold values from 0 to 5, each once within a row
- pivot_states: bfloat16 [6, 2048], replicated, may hold values from -480 to 480
- query_weight: bfloat16 [2048, 2048], P(None, 'tensor'), may hold values from -0.125 to 0.125
- key_weight: bfloat16 [2048, 2048], P(None, 'tensor'), may hold values from -0.125 to 0.125
- value_weight: bfloat16 [2048, 2048], P(None, 'tensor'), may hold values from -0.125 to 0.125
- out_weight: bfloat16 [2048, 2048], P('tensor'), may hold values from -0.125 to 0.125
Outputs:
- encoded_states: bfloat16 [2048, 2048], P(('groups', 'expert'), 'tensor'), parts along dimension 0
- decoder_states: bfloat16 [384, 2048], P(('groups', 'expert')), parts along dimension 0
There are 2 independent parts, one for each index of `groups`. A program takes and returns all parts, laid end to end along the dimension named above; an argument that names none is the same for every part. Nothing has to cross between parts.
Inputs may be any that keep to these rules, and one draw needn't show every extreme that they name: `routes`: each token names two different experts; among the 256 tokens of one block no expert is named more than 256 times. `lengths`: each row sums to 256. `lang_ids`: each row names every pivot language once.
All inputs are finite; a program needn't handle non-finite values.
Results may differ from a plain program's by a relative error of at most 0.012.
Values may be sent and summed in bfloat16 or wider, within the bound.
A program may use at most 128 MiB of HBM per device.

v0:
```python
import jax
import jax.numpy as jnp
from jax import lax
from jax.sharding import PartitionSpec as P

HD = 128
EPSILON = 1e-05
NEGATIVE = -1e30


def normalize(values):
    values = values.astype(jnp.float32)
    center = jnp.mean(values, axis=-1, keepdims=True)
    shifted = values - center
    spread = jnp.mean(shifted * shifted, axis=-1, keepdims=True)
    return shifted * lax.rsqrt(spread + EPSILON)


def route_tables(routes, experts, capacity):
    tok_count = routes.shape[0]
    expert_iota = jnp.arange(experts, dtype=jnp.int32)
    chosen = routes[:, :, None] == expert_iota[None, None, :]
    flat_chosen = chosen.reshape(tok_count * 2, experts).astype(jnp.int32)
    before = jnp.cumsum(flat_chosen, axis=0) - flat_chosen
    slots = jnp.sum(before * flat_chosen, axis=1).reshape(tok_count, 2)
    slot_iota = jnp.arange(capacity, dtype=jnp.int32)
    placed = chosen[:, :, :, None] & (slots[:, :, None, None] == slot_iota[None, None, None, :])
    return (chosen, placed.reshape(tok_count, 2, experts * capacity).astype(jnp.bfloat16))


def project_pair(key_weight, value_weight):

    def project(totals, shard_part, offset):
        return (
            jnp.dot(shard_part, key_weight, preferred_element_type=jnp.float32),
            jnp.dot(shard_part, value_weight, preferred_element_type=jnp.float32),
        )

    return project


def shards(
    source_states,
    routes,
    router_weight,
    fc1_weight,
    fc2_weight,
    lengths,
    lang_ids,
    pivot_states,
    query_weight,
    key_weight,
    value_weight,
    out_weight,
):
    tok_count, model_width = source_states.shape
    experts = router_weight.shape[1]
    capacity = 4 * tok_count // experts
    tensor_count = lax.axis_size("tensor")
    column_width = model_width // tensor_count
    column_start = lax.axis_index("tensor") * column_width
    normed = normalize(source_states).astype(jnp.bfloat16)
    logits = jnp.dot(normed, router_weight, preferred_element_type=jnp.float32)
    chosen, placed = route_tables(routes, experts, capacity)
    pair_logits = jnp.sum(jnp.where(chosen, logits[:, None, :], 0.0), axis=2)
    gate_values = jax.nn.sigmoid(pair_logits - pair_logits[:, ::-1])
    occupied = jnp.sum(placed, axis=1)
    outgoing = jnp.einsum("ts,td->sd", occupied, normed, preferred_element_type=jnp.float32)
    outgoing = outgoing.astype(jnp.bfloat16).reshape(experts, capacity, model_width)
    weight_in = fc1_weight[0]
    weight_back = fc2_weight[0]
    arrived = lax.all_to_all(outgoing, "expert", split_axis=0, concat_axis=0, tiled=True)
    row_block = arrived.reshape(-1, model_width)
    hidden = jnp.maximum(
        jnp.dot(row_block, weight_in, preferred_element_type=jnp.float32), 0.0
    ).astype(jnp.bfloat16)
    partial_value = jnp.dot(hidden, weight_back, preferred_element_type=jnp.float32).astype(
        jnp.bfloat16
    )
    partials = partial_value.reshape(arrived.shape)
    zeroed = jnp.zeros((tok_count, key_weight.shape[1]), jnp.float32)
    project = project_pair(key_weight, value_weight)
    own_cols = lax.dynamic_slice_in_dim(source_states, column_start, column_width, 1).astype(
        jnp.float32
    )
    widened = partials.astype(jnp.float32)
    summed = lax.psum_scatter(
        widened.astype(jnp.bfloat16), "tensor", scatter_dimension=2, tiled=True
    )
    returned_rows = lax.all_to_all(summed, "expert", split_axis=0, concat_axis=0, tiled=True)
    picked = jnp.einsum(
        "tks,sd->tkd",
        placed,
        returned_rows.reshape(experts * capacity, column_width),
        preferred_element_type=jnp.float32,
    )
    encoded = (own_cols + jnp.sum(gate_values[:, :, None] * picked, axis=1)).astype(jnp.bfloat16)
    key_sum, value_sum = project(
        (zeroed, zeroed), lax.all_gather(encoded, "tensor", axis=1, tiled=True), jnp.int32(0)
    )
    key_cache = key_sum.astype(jnp.bfloat16)
    value_cache = value_sum.astype(jnp.bfloat16)
    query_count = lengths.shape[1]
    pivot_count = pivot_states.shape[0]
    row_count = query_count * pivot_count
    query_ends = jnp.cumsum(lengths[0])
    positions = jnp.arange(tok_count, dtype=jnp.int32)
    key_owner = jnp.sum((positions[:, None] >= query_ends[None, :]).astype(jnp.int32), axis=1)
    row_owner = jnp.arange(row_count, dtype=jnp.int32) // pivot_count
    allowed = row_owner[:, None] == key_owner[None, :]
    language_pick = (
        lang_ids.reshape(-1)[:, None] == jnp.arange(pivot_count, dtype=jnp.int32)[None, :]
    ).astype(jnp.bfloat16)
    decoder_in = jnp.dot(language_pick, pivot_states, preferred_element_type=jnp.float32).astype(
        jnp.bfloat16
    )
    queries = jnp.dot(decoder_in, query_weight, preferred_element_type=jnp.float32).astype(
        jnp.bfloat16
    )
    head_local = queries.shape[1] // HD
    query_heads = queries.reshape(row_count, head_local, HD)
    key_heads = key_cache.reshape(tok_count, head_local, HD)
    value_heads = value_cache.reshape(tok_count, head_local, HD)
    scores = jnp.einsum(
        "rhe,the->hrt", query_heads, key_heads, preferred_element_type=jnp.float32
    ) * HD ** (-0.5)
    scores = jnp.where(allowed[None], scores, NEGATIVE)
    row_max = jnp.max(scores, axis=2, keepdims=True)
    weights = jnp.exp(scores - row_max)
    attention = (weights / jnp.sum(weights, axis=2, keepdims=True)).astype(jnp.bfloat16)
    context = jnp.einsum(
        "hrt,the->rhe", attention, value_heads, preferred_element_type=jnp.float32
    ).astype(jnp.bfloat16)
    partial_out = jnp.dot(
        context.reshape(row_count, head_local * HD), out_weight, preferred_element_type=jnp.float32
    )
    attn_total = lax.psum(partial_out.astype(jnp.bfloat16), "tensor").astype(jnp.float32)
    decoded = normalize(decoder_in.astype(jnp.float32) + attn_total).astype(jnp.bfloat16)
    return (encoded, decoded)


def solution(mesh):
    in_specs = (
        P(("groups", "expert"), None),
        P(("groups", "expert"), None),
        P(),
        P("expert", None, "tensor"),
        P("expert", "tensor", None),
        P(("groups", "expert"), None),
        P(("groups", "expert"), None),
        P(),
        P(None, "tensor"),
        P(None, "tensor"),
        P(None, "tensor"),
        P("tensor", None),
    )
    out_specs = (P(("groups", "expert"), "tensor"), P(("groups", "expert"), None))
    return jax.shard_map(shards, mesh=mesh, in_specs=in_specs, out_specs=out_specs, check_vma=False)
```

profile of v0, /device:TPU:0, one launch (start us, length us, event | category | flops | bytes accessed | tf_op | source)
XLA Modules:
  0.0 283.3 jit_solution(7772362713964266053)
XLA Ops:
  7.2 0.0 reduce-scatter.2.cloned.1.call-start
  7.2 1.0 copy.39
  8.2 0.1 eq.95
  8.4 0.1 eq.91
  8.5 0.7 iota_compare_fusion.6
  9.2 1.2 reduce-window.18
  10.4 0.2 slice_reduce_fusion
  10.7 0.2 reduce-window.19
  10.8 0.1 add_bitcast_fusion
  10.9 0.1 eq.99
  11.1 0.1 copy.41
  11.2 0.2 iota_compare_fusion
  11.3 1.3 fusion.32
  12.7 2.1 copy.42
  14.7 0.2 convert_reduce_fusion
  15.0 0.4 fusion.14
  15.4 0.4 copy-done.2
  15.8 1.4 convolution_convert_fusion
  17.2 99.4 %all_to_all.10 = bf16[4,256,2048]{2,1,0:T(8,128)(2,1)} all-to-all(bf16[4,256,2048]{2,1,0:T(8,128)(2,1)S(1)} %bitcast.88), channel_id=1, replica_groups=mesh['groups'=2,'expert'=4,'tensor'=4] {'expert'}, dimensions={0} | all-to-all | bytes 8388608 | tf_op jit(solution)/shard_map/all_to_all | solution.py:72
  116.5 25.4 %fusion.7 = bf16[1024,2048]{1,0:T(8,128)(2,1)} fusion(bf16[1,2048,2048]{2,1,0:T(8,128)(2,1)} %param.16, bf16[1024,2048]{1,0:T(8,128)(2,1)} %bitcast.90, bf16[1,2048,2048]{2,1,0:T(8,128)(2,1)} %param.15), kind=kOutput, calls=%fused_computation.6 | convolution fusion | flops 17186160640 | bytes 25165824 | tf_op jit(solution)/shard_map/dot_general | solution.py:77
  141.9 0.0 reduce-scatter.2.cloned.1.call-update
  142.0 44.0 %reduce-scatter.2.cloned.1.call-done = bf16[4,256,512]{2,1,0:T(8,128)(2,1)} async-done(((bf16[4,256,2048]{2,1,0:T(8,128)(2,1)}), bf16[4,256,512]{2,1,0:T(8,128)(2,1)}) %reduce-scatter.2.cloned.1.call-update) | async-done | bytes 1048592 | tf_op jit(solution)/shard_map/reduce_scatter | solution.py:87
  186.0 4.6 %all-to-all-start.1 = ((bf16[4,256,512]{2,1,0:T(8,128)(2,1)}), bf16[4,256,512]{2,1,0:T(8,128)(2,1)}, u32[]{:S(2)}, u32[]{:S(2)}) async-start(bf16[4,256,512]{2,1,0:T(8,128)(2,1)} %reduce-scatter.2.cloned.1.call-done), calls=%async_computation.2 | async-start | bytes 2097152 | tf_op jit(solution)/shard_map/all_to_all | solution.py:90
  190.6 0.4 fusion.54
  191.1 0.1 rev.3
  191.2 25.2 %all-to-all-done.1 = bf16[4,256,512]{2,1,0:T(8,128)(2,1)} async-done(((bf16[4,256,512]{2,1,0:T(8,128)(2,1)}), bf16[4,256,512]{2,1,0:T(8,128)(2,1)}, u32[]{:S(2)}, u32[]{:S(2)}) %all-to-all-start.1) | async-done | bytes 1048608 | tf_op jit(solution)/shard_map/all_to_all | solution.py:90
  216.4 2.3 fusion.22
  218.7 0.8 add_convert_fusion
  219.5 0.0 all-gather.2.cloned.1.call-update
  219.5 0.0 all-reduce.2.cloned.1.call-start
  219.5 0.1 eq.103
  219.6 0.2 reduce-window.20
  219.8 0.1 convert_reduce_fusion.1
  219.9 0.1 broadcast_compare_fusion
  220.0 0.2 convolution_convert_fusion.2
  220.3 2.1 fusion.31
  222.3 12.2 %all-gather.2.cloned.1.call-done = bf16[256,2048]{1,0:T(8,128)(2,1)} async-done(((bf16[256,512]{1,0:T(8,128)(2,1)}), bf16[256,2048]{1,0:T(8,128)(2,1)}) %all-gather.2.cloned.1.call-update) | async-done | bytes 1048592 | tf_op jit(solution)/shard_map/all_gather | solution.py:99
  234.5 2.1 fusion.27
  236.6 0.2 fusion.28
  236.8 0.2 fusion.56
  237.0 0.7 fusion.26
  237.8 0.4 fusion.30
  238.1 2.8 convolution_convert_fusion.1
  240.9 0.0 all-reduce.2.cloned.1.call-update
  240.9 31.8 %all-reduce.2.cloned.1.call-done = bf16[48,2048]{1,0:T(8,128)(2,1)} async-done(((bf16[48,2048]{1,0:T(8,128)(2,1)}), bf16[48,2048]{1,0:T(8,128)(2,1)}) %all-reduce.2.cloned.1.call-update) | async-done | bytes 196624 | tf_op jit(solution)/shard_map/psum | solution.py:137
  272.8 1.1 fusion.37
  273.8 1.1 multiply_reduce_fusion
  275.0 1.7 multiply_convert_fusion
  (29 shorter events, 0.2 us)
Async XLA Ops:
  7.2 227.4 %copy-start = (bf16[2048,512]{1,0:T(8,128)(2,1)S(1)}, bf16[2048,512]{1,0:T(8,128)(2,1)}, u32[]{:S(2)}) copy-start(bf16[2048,512]{1,0:T(8,128)(2,1)} %param.21) | copy-start | bytes 6291460
  7.2 7.6 %copy-start.1 = (bf16[256,2048]{1,0:T(8,128)(2,1)S(1)}, bf16[256,2048]{1,0:T(8,128)(2,1)}, u32[]{:S(2)}) copy-start(bf16[256,2048]{1,0:T(8,128)(2,1)} %param.12) | copy-start | bytes 3145732
  7.2 178.8 %reduce-scatter.2.cloned.1.call-start = ((), (), s32[]{:S(2)}) async-start(), calls=%async_computation.3 | async-start | bytes 5242880 | tf_op jit(solution)/shard_map/reduce_scatter | solution.py:87
  14.7 1.0 copy-start.2
  141.9 48.6 %copy-start.8 = (bf16[2048,4]{0,1:T(4,128)(2,1)S(1)}, bf16[2048,4]{0,1:T(4,128)(2,1)}, u32[]{:S(2)}) copy-start(bf16[2048,4]{0,1:T(4,128)(2,1)} %param.14) | copy-start | bytes 49156
  141.9 49.1 %copy-start.4 = (s32[256,2]{0,1:T(2,128)S(1)}, s32[256,2]{0,1:T(2,128)}, u32[]{:S(2)}) copy-start(s32[256,2]{0,1:T(2,128)} %param.13) | copy-start | bytes 6148
  186.0 30.4 %all-to-all-start.1 = ((bf16[4,256,512]{2,1,0:T(8,128)(2,1)}), bf16[4,256,512]{2,1,0:T(8,128)(2,1)}, u32[]{:S(2)}, u32[]{:S(2)}) async-start(bf16[4,256,512]{2,1,0:T(8,128)(2,1)} %reduce-scatter.2.cloned.1.call-done), calls=%async_computation.2 | async-start | bytes 2097152 | tf_op jit(solution)/shard_map/all_to_all | solution.py:90
  190.6 44.0 %all-gather.2.cloned.1.call-start = ((), (), s32[]{:S(2)}) async-start(), calls=%async_computation.4 | async-start | bytes 1310720 | tf_op jit(solution)/shard_map/all_gather | solution.py:99
  191.2 28.4 %copy-start.5 = (s32[8,6]{1,0:T(8,128)S(1)}, s32[8,6]{1,0:T(8,128)}, u32[]{:S(2)}) copy-start(s32[8,6]{1,0:T(8,128)} %param.18) | copy-start | bytes 580
  191.2 28.5 %copy-start.9 = (s32[1,8]{1,0:T(1,128)S(1)}, s32[1,8]{1,0:T(1,128)}, u32[]{:S(2)}) copy-start(s32[1,8]{1,0:T(1,128)} %param.17) | copy-start | bytes 100
  191.2 28.8 %copy-start.3 = (bf16[6,2048]{1,0:T(8,128)(2,1)S(1)}, bf16[6,2048]{1,0:T(8,128)(2,1)}, u32[]{:S(2)}) copy-start(bf16[6,2048]{1,0:T(8,128)(2,1)} %param.19) | copy-start | bytes 73732
  219.5 53.3 %all-reduce.2.cloned.1.call-start = ((), (), s32[]{:S(2)}) async-start(), calls=%async_computation.5 | async-start | bytes 393216 | tf_op jit(solution)/shard_map/psum | solution.py:137
  234.5 2.5 copy-start.6
  234.5 2.5 copy-start.7
Sparse Core Ops, SparseCore 0:
  142.0 43.8 reduce-scatter.1
  219.6 14.8 all-gather.1
  241.0 31.6 all-reduce.1
where the time goes:
time: 284 us; the launch traced here: 283 us
  waiting for transfers between devices  113 us (40%)
  blocking collectives  99.4 us (35%)
  matrix products  37.9 us (13%)
  between operations  14 us (5%)
  other arithmetic  9.69 us (3%)
  starting transfers between devices  4.68 us (2%)
  local copies, waits for them, and re-layouts  4.36 us (2%)
    all_to_all x1, blocking collectives, shards(): lax.all_to_all(outgoing, 'expert', split_axis=0, concat_axis=0, tiled=True)  99.4 us
    reduce_scatter x1, waiting for transfers between devices, shards(): lax.psum_scatter(widened.astype(jnp.bfloat16), 'tensor', scatter_dimensio...  44 us
    psum x1, waiting for transfers between devices, shards(): lax.psum(partial_out.astype(jnp.bfloat16), 'tensor').astype(jnp.float32)  31.8 us
    dot_general x1, matrix products, shards(): jnp.dot(hidden, weight_back, preferred_element_type=jnp.float32)  25.4 us
    all_to_all x1, waiting for transfers between devices, shards(): lax.all_to_all(summed, 'expert', split_axis=0, concat_axis=0, tiled=True)  25.2 us
    all_gather x1, waiting for transfers between devices, shards(): lax.all_gather(encoded, 'tensor', axis=1, tiled=True)  12.2 us
  transfers between devices with their start and end apart: 4, of which 4 were waited for; matrix products, arithmetic and copies ran while one was open for 1% of the time, Pallas kernels for 0%

commit v1 on v0

--- a/solution.py
+++ b/solution.py
@@ -134,7 +134,9 @@
     partial_out = jnp.dot(
         context.reshape(row_count, head_local * HD), out_weight, preferred_element_type=jnp.float32
     )
-    attn_total = lax.psum(partial_out.astype(jnp.bfloat16), "tensor").astype(jnp.float32)
+    attn_total = jnp.sum(lax.all_gather(partial_out.astype(jnp.bfloat16), "tensor"), axis=0).astype(
+        jnp.float32
+    )
     decoded = normalize(decoder_in.astype(jnp.float32) + attn_total).astype(jnp.bfloat16)
     return (encoded, decoded)
 

time: 284 us -> 259 us (0.912)
  waiting for transfers between devices: 113 us -> 81.5 us
  blocking collectives: 99.4 us -> 108 us
    psum x1 -> x0, waiting for transfers between devices: 31.8 us -> none  [shards(): lax.psum(partial_out.astype(jnp.bfloat16), 'tensor').astype(jnp.float32)]
    all_gather x0 -> x1, blocking collectives: none -> 9.05 us  [shards(): lax.all_gather(partial_out.astype(jnp.bfloat16), 'tensor')]
  transfers between devices with their start and end apart: 4 -> 3, of which waited for: 4 -> 3; matrix products, arithmetic and copies ran while one was open for 1% -> 1% of each run, Pallas kernels for 0% -> 0%
where the time goes in v1:
time: 259 us
  blocking collectives  108 us (42%)
  waiting for transfers between devices  81.5 us (31%)
  matrix products  37.2 us (14%)
  between operations  14.3 us (6%)
  other arithmetic  8.18 us (3%)
  starting transfers between devices  4.64 us (2%)
  local copies, waits for them, and re-layouts  4.36 us (2%)
    all_to_all x1, blocking collectives, shards(): lax.all_to_all(outgoing, 'expert', split_axis=0, concat_axis=0, tiled=True)  99.4 us
    reduce_scatter x1, waiting for transfers between devices, shards(): lax.psum_scatter(widened.astype(jnp.bfloat16), 'tensor', scatter_dimensio...  44 us
    dot_general x1, matrix products, shards(): jnp.dot(hidden, weight_back, preferred_element_type=jnp.float32)  25.4 us
    all_to_all x1, waiting for transfers between devices, shards(): lax.all_to_all(summed, 'expert', split_axis=0, concat_axis=0, tiled=True)  25.2 us
    all_gather x1, waiting for transfers between devices, shards(): lax.all_gather(encoded, 'tensor', axis=1, tiled=True)  12.2 us
    all_gather x1, blocking collectives, shards(): lax.all_gather(partial_out.astype(jnp.bfloat16), 'tensor')  9.05 us
  transfers between devices with their start and end apart: 3, of which 3 were waited for; matrix products, arithmetic and copies ran while one was open for 1% of the time, Pallas kernels for 0%

profile of v1, /device:TPU:0, one launch (start us, length us, event | category | flops | bytes accessed | tf_op | source)
XLA Modules:
  0.0 258.5 jit_solution(7010802427442146056)
XLA Ops:
  7.2 0.0 copy-start
  7.2 0.0 reduce-scatter.2.cloned.1.call-start
  7.2 1.0 copy.39
  8.2 0.1 eq.95
  8.4 0.1 eq.91
  8.5 0.7 iota_compare_fusion.6
  9.2 1.2 reduce-window.18
  10.4 0.2 slice_reduce_fusion
  10.7 0.2 reduce-window.19
  10.8 0.1 add_bitcast_fusion
  10.9 0.1 eq.99
  11.1 0.1 copy.41
  11.2 0.2 iota_compare_fusion
  11.3 1.3 fusion.32
  12.7 2.1 copy.42
  14.7 0.2 convert_reduce_fusion
  15.0 0.4 fusion.14
  15.4 0.4 copy-done.2
  15.8 1.4 convolution_convert_fusion
  17.2 99.4 %all_to_all.10 = bf16[4,256,2048]{2,1,0:T(8,128)(2,1)} all-to-all(bf16[4,256,2048]{2,1,0:T(8,128)(2,1)S(1)} %bitcast.89), channel_id=1, replica_groups=mesh['groups'=2,'expert'=4,'tensor'=4] {'expert'}, dimensions={0} | all-to-all | bytes 8388608 | tf_op jit(solution)/shard_map/all_to_all | solution.py:72
  116.6 25.4 %fusion.7 = bf16[1024,2048]{1,0:T(8,128)(2,1)} fusion(bf16[1,2048,2048]{2,1,0:T(8,128)(2,1)} %param.16, bf16[1024,2048]{1,0:T(8,128)(2,1)} %bitcast.91, bf16[1,2048,2048]{2,1,0:T(8,128)(2,1)} %param.15), kind=kOutput, calls=%fused_computation.6 | convolution fusion | flops 17186160640 | bytes 25165824 | tf_op jit(solution)/shard_map/dot_general | solution.py:77
  141.9 0.0 reduce-scatter.2.cloned.1.call-update
  142.0 44.0 %reduce-scatter.2.cloned.1.call-done = bf16[4,256,512]{2,1,0:T(8,128)(2,1)} async-done(((bf16[4,256,2048]{2,1,0:T(8,128)(2,1)}), bf16[4,256,512]{2,1,0:T(8,128)(2,1)}) %reduce-scatter.2.cloned.1.call-update) | async-done | bytes 1048592 | tf_op jit(solution)/shard_map/reduce_scatter | solution.py:87
  186.0 4.6 %all-to-all-start.1 = ((bf16[4,256,512]{2,1,0:T(8,128)(2,1)}), bf16[4,256,512]{2,1,0:T(8,128)(2,1)}, u32[]{:S(2)}, u32[]{:S(2)}) async-start(bf16[4,256,512]{2,1,0:T(8,128)(2,1)} %reduce-scatter.2.cloned.1.call-done), calls=%async_computation.2 | async-start | bytes 2097152 | tf_op jit(solution)/shard_map/all_to_all | solution.py:90
  190.6 0.4 fusion.54
  191.1 0.1 rev.3
  191.2 25.2 %all-to-all-done.1 = bf16[4,256,512]{2,1,0:T(8,128)(2,1)} async-done(((bf16[4,256,512]{2,1,0:T(8,128)(2,1)}), bf16[4,256,512]{2,1,0:T(8,128)(2,1)}, u32[]{:S(2)}, u32[]{:S(2)}) %all-to-all-start.1) | async-done | bytes 1048608 | tf_op jit(solution)/shard_map/all_to_all | solution.py:90
  216.4 2.3 fusion.22
  218.7 0.8 add_convert_fusion
  219.5 0.0 all-gather.3.cloned.1.call-update
  219.5 0.1 eq.103
  219.6 0.2 reduce-window.20
  219.8 0.1 convert_reduce_fusion.1
  219.9 0.1 broadcast_compare_fusion
  220.0 0.2 convolution_convert_fusion.2
  220.2 2.1 fusion.31
  222.3 12.2 %all-gather.3.cloned.1.call-done = bf16[256,2048]{1,0:T(8,128)(2,1)} async-done(((bf16[256,512]{1,0:T(8,128)(2,1)}), bf16[256,2048]{1,0:T(8,128)(2,1)}) %all-gather.3.cloned.1.call-update) | async-done | bytes 1048592 | tf_op jit(solution)/shard_map/all_gather | solution.py:99
  234.5 2.1 fusion.27
  236.6 0.2 fusion.28
  236.8 0.2 fusion.56
  237.0 0.7 fusion.26
  237.7 0.4 fusion.30
  238.1 2.1 convolution_convert_fusion.1
  240.2 9.1 %all-gather = bf16[192,2048]{1,0:T(8,128)(2,1)} all-gather(bf16[48,2048]{1,0:T(8,128)(2,1)S(1)} %convolution_convert_fusion.1), channel_id=2, replica_groups=mesh['groups'=2,'expert'=4,'tensor'=4] {'tensor'}, dimensions={0}, use_global_device_ids=true | all-gather | bytes 983040 | tf_op jit(solution)/shard_map/all_gather | solution.py:137
  249.2 1.3 reduce_sum.116
  250.5 0.2 fusion.37
  250.7 0.2 multiply_reduce_fusion
  250.9 0.8 multiply_convert_fusion
  (28 shorter events, 0.2 us)
Async XLA Ops:
  7.2 227.3 %copy-start = (bf16[2048,512]{1,0:T(8,128)(2,1)S(1)}, bf16[2048,512]{1,0:T(8,128)(2,1)}, u32[]{:S(2)}) copy-start(bf16[2048,512]{1,0:T(8,128)(2,1)} %param.21) | copy-start | bytes 6291460
  7.2 7.6 %copy-start.1 = (bf16[256,2048]{1,0:T(8,128)(2,1)S(1)}, bf16[256,2048]{1,0:T(8,128)(2,1)}, u32[]{:S(2)}) copy-start(bf16[256,2048]{1,0:T(8,128)(2,1)} %param.12) | copy-start | bytes 3145732
  7.2 178.8 %reduce-scatter.2.cloned.1.call-start = ((), (), s32[]{:S(2)}) async-start(), calls=%async_computation.3 | async-start | bytes 5242880 | tf_op jit(solution)/shard_map/reduce_scatter | solution.py:87
  14.7 1.0 copy-start.2
  141.9 48.7 %copy-start.8 = (bf16[2048,4]{0,1:T(4,128)(2,1)S(1)}, bf16[2048,4]{0,1:T(4,128)(2,1)}, u32[]{:S(2)}) copy-start(bf16[2048,4]{0,1:T(4,128)(2,1)} %param.14) | copy-start | bytes 49156
  141.9 49.1 %copy-start.4 = (s32[256,2]{0,1:T(2,128)S(1)}, s32[256,2]{0,1:T(2,128)}, u32[]{:S(2)}) copy-start(s32[256,2]{0,1:T(2,128)} %param.13) | copy-start | bytes 6148
  186.0 30.4 %all-to-all-start.1 = ((bf16[4,256,512]{2,1,0:T(8,128)(2,1)}), bf16[4,256,512]{2,1,0:T(8,128)(2,1)}, u32[]{:S(2)}, u32[]{:S(2)}) async-start(bf16[4,256,512]{2,1,0:T(8,128)(2,1)} %reduce-scatter.2.cloned.1.call-done), calls=%async_computation.2 | async-start | bytes 2097152 | tf_op jit(solution)/shard_map/all_to_all | solution.py:90
  190.6 43.9 %all-gather.3.cloned.1.call-start = ((), (), s32[]{:S(2)}) async-start(), calls=%async_computation.4 | async-start | bytes 1310720 | tf_op jit(solution)/shard_map/all_gather | solution.py:99
  191.2 28.3 %copy-start.5 = (s32[8,6]{1,0:T(8,128)S(1)}, s32[8,6]{1,0:T(8,128)}, u32[]{:S(2)}) copy-start(s32[8,6]{1,0:T(8,128)} %param.18) | copy-start | bytes 580
  191.2 28.4 %copy-start.9 = (s32[1,8]{1,0:T(1,128)S(1)}, s32[1,8]{1,0:T(1,128)}, u32[]{:S(2)}) copy-start(s32[1,8]{1,0:T(1,128)} %param.17) | copy-start | bytes 100
  191.2 28.8 %copy-start.3 = (bf16[6,2048]{1,0:T(8,128)(2,1)S(1)}, bf16[6,2048]{1,0:T(8,128)(2,1)}, u32[]{:S(2)}) copy-start(bf16[6,2048]{1,0:T(8,128)(2,1)} %param.19) | copy-start | bytes 73732
  234.5 2.5 copy-start.6
  234.5 2.5 copy-start.7
Sparse Core Ops, SparseCore 0:
  142.1 43.8 reduce-scatter.1
  219.6 14.8 all-gather.2
